TPU v7x, 32 devices: a whole 2x2x4 slice. The times are simulated.
32 devices in a mesh: blocks: 8 (over z, y), filt: 4 (over x, core).
Axes of the slice: x: 2, y: 2, z: 4, core: 2. Of those that a mesh axis runs over, the one named last changes fastest.
Arguments:
- volume: bfloat16 [64, 4, 64, 128], P(None, None, 'blocks'), may hold values from -6 to 6
- w_first: bfloat16 [3, 3, 64, 64], P(None, None, 'filt'), may hold values from -0.25 to 0.25
- w_second: bfloat16 [3, 3, 3, 64, 64], P(None, None, None, 'filt'), may hold values from -0.15625 to 0.15625
- cotangent: bfloat16 [64, 4, 64, 128], P('filt', None, 'blocks'), may hold values from -6 to 6
Outputs:
- output: bfloat16 [64, 4, 64, 128], P('filt', None, 'blocks')
- input_grad: bfloat16 [64, 4, 64, 128], P('filt', None, 'blocks')
- first_grad: float32 [3, 3, 64, 64], P(None, None, 'filt')
- second_grad: float32 [3, 3, 3, 64, 64], P(None, None, None, 'filt')
All inputs are finite; a program needn't handle non-finite values.
Results may differ from a plain program's by a relative error of at most 0.012.
Values may be sent and summed in bfloat16 or wider, within the bound.
A program may use at most 64 MiB of HBM per device.

v0:
```python
import math

import jax
import jax.numpy as jnp
from jax import lax
from jax.sharding import PartitionSpec as P


def extended(block, sides, width):
    for axis, dim in sides:
        count = lax.axis_size(axis)
        forward = [(i, i + 1) for i in range(count - 1)]
        backward = [(target, source) for source, target in forward]
        low = lax.ppermute(
            lax.slice_in_dim(block, block.shape[dim] - width, None, axis=dim), axis, forward
        )
        high = lax.ppermute(lax.slice_in_dim(block, 0, width, axis=dim), axis, backward)
        block = jnp.concatenate([low, block, high], axis=dim)
    return block


def correlate(padded, kernel, stride, out_depth, out_rows, out_cols):
    summed = None
    for a in range(kernel.shape[0]):
        for b in range(kernel.shape[1]):
            for c in range(kernel.shape[2]):
                window = padded[
                    :,
                    a * stride : a * stride + out_depth,
                    b * stride : b * stride + out_rows,
                    c * stride : c * stride + out_cols,
                ]
                product = jnp.einsum(
                    "oi,izyx->ozyx", kernel[a, b, c], window, preferred_element_type=jnp.float32
                )
                summed = product if summed is None else summed + product
    return summed


def kernel_grads(left, padded, taps, stride):
    out_depth, out_rows, out_cols = (left.shape[1], left.shape[2], left.shape[3])
    planes = []
    for a in range(taps[0]):
        lines = []
        for b in range(taps[1]):
            entries = []
            for c in range(taps[2]):
                window = padded[
                    :,
                    a * stride : a * stride + out_depth,
                    b * stride : b * stride + out_rows,
                    c * stride : c * stride + out_cols,
                ]
                entries.append(
                    jnp.einsum("ozyx,izyx->oi", left, window, preferred_element_type=jnp.float32)
                )
            lines.append(jnp.stack(entries))
        planes.append(jnp.stack(lines))
    return jnp.stack(planes)


def flipped(kernel):
    return jnp.swapaxes(jnp.flip(kernel, axis=(0, 1, 2)), 3, 4)


def silu_slope(pre):
    sigma = jax.nn.sigmoid(pre)
    return sigma * (1.0 + pre * (1.0 - sigma))


def per_device(volume, w_first, w_second, cotangent):
    z_cells, y_rows, x_cells = (volume.shape[1], volume.shape[2], volume.shape[3])
    block_count = lax.axis_size("blocks")
    block_index = lax.axis_index("blocks")
    first_kernel = w_first[None]
    volume_halo = extended(volume, (("blocks", 2),), 3)
    volume_wide = jnp.pad(volume_halo, ((0, 0), (0, 0), (0, 0), (1, 1)))
    pre_wide = correlate(volume_wide, first_kernel, 1, z_cells, y_rows + 4, x_cells)
    global_row = block_index * y_rows - 2 + jnp.arange(y_rows + 4, dtype=jnp.int32)
    inside = (global_row >= 0) & (global_row < y_rows * block_count)
    hidden_wide = jnp.where(inside[None, None, :, None], jax.nn.silu(pre_wide), 0.0).astype(
        jnp.bfloat16
    )
    hidden_rim = lax.all_gather(hidden_wide, "filt", axis=0, tiled=True)
    pre = pre_wide[:, :, 2:-2]
    volume_pad = volume_wide[:, :, 2:-2]
    hidden_pad = jnp.pad(hidden_rim, ((0, 0), (2, 2), (0, 0), (2, 2)))
    output = correlate(hidden_pad, w_second, 2, z_cells, y_rows, x_cells).astype(jnp.bfloat16)
    second_local = kernel_grads(cotangent, hidden_pad, (3, 3, 3), 2)
    grad_rim = extended(cotangent, (("blocks", 2),), 2)
    grad_pad = jnp.pad(grad_rim, ((0, 0), (2, 2), (0, 0), (2, 2)))
    partial_hidden = correlate(grad_pad, flipped(w_second), 2, z_cells, y_rows, x_cells)
    hidden_grad = lax.psum_scatter(partial_hidden, "filt", scatter_dimension=0, tiled=True)
    pre_grad = (hidden_grad * silu_slope(pre)).astype(jnp.bfloat16)
    first_local = kernel_grads(pre_grad, volume_pad, (1, 3, 3), 1)[0]
    pre_rim = extended(pre_grad, (("blocks", 2),), 1)
    pre_pad = jnp.pad(pre_rim, ((0, 0), (0, 0), (0, 0), (1, 1)))
    partial_input = correlate(pre_pad, flipped(first_kernel), 1, z_cells, y_rows, x_cells)
    input_grad = lax.psum_scatter(
        partial_input.astype(jnp.bfloat16), "filt", scatter_dimension=0, tiled=True
    )
    factor = 1.0 / math.sqrt(z_cells * y_rows * block_count * x_cells)
    first_grad, second_grad = lax.psum((first_local * factor, second_local * factor), "blocks")
    return (output, input_grad, first_grad, second_grad)


def solution(mesh):
    return jax.shard_map(
        per_device,
        mesh=mesh,
        in_specs=(
            P(None, None, "blocks", None),
            P(None, None, "filt", None),
            P(None, None, None, "filt", None),
            P("filt", None, "blocks", None),
        ),
        out_specs=(
            P("filt", None, "blocks", None),
            P("filt", None, "blocks", None),
            P(None, None, "filt", None),
            P(None, None, None, "filt", None),
        ),
        check_vma=False,
    )
```

profile of v0, /device:TPU:0, one launch (start us, length us, event | category | flops | bytes accessed | tf_op | source)
XLA Modules:
  0.0 167.9 jit_solution(5440556789084541919)
XLA Ops:
  8.0 1.0 copy.11
  9.0 5.0 %collective-permute-start.2 = (bf16[16,4,2,128]{3,0,2,1:T(8,128)(2,1)S(1)}, bf16[16,4,2,128]{3,0,2,1:T(8,128)(2,1)S(1)}, u32[]{:S(2)}, u32[]{:S(2)}) collective-permute-start(bf16[16,4,2,128]{3,0,2,1:T(8,128)(2,1)S(1)} %get-tuple-element.45), channel_id=1, source_target_pairs={{0,4},{4,8},{8,12},{12,16},{16,20},{20,24},{24,28},{1,5},{5,9},{9,... | collective-permute-start | bytes 98312 | tf_op jit(solution)/shard_map/ppermute | solution.py:14
  14.1 1.4 collective-permute-start.3
  15.5 1.4 fusion.255
  17.0 5.4 %collective-permute-start = (bf16[64,4,3,128]{3,0,2,1:T(8,128)(2,1)S(1)}, bf16[64,4,3,128]{3,0,2,1:T(8,128)(2,1)}, u32[]{:S(2)}, u32[]{:S(2)}) collective-permute-start(bf16[64,4,3,128]{3,0,2,1:T(8,128)(2,1)S(1)} %copy.344), channel_id=1, source_target_pairs={{0,4},{4,8},{8,12},{12,16},{16,20},{20,24},{24,28},{1,5},{5,9},{9,... | collective-permute-start | bytes 589832 | tf_op jit(solution)/shard_map/ppermute | solution.py:14
  22.4 1.3 collective-permute-start.1
  33.9 1.4 fusion.7
  40.6 8.8 %all_gather.3 = bf16[64,4,12,128]{3,0,2,1:T(8,128)(2,1)S(1)} all-gather(bf16[16,4,12,128]{3,0,2,1:T(8,128)(2,1)S(1)} %get-tuple-element.47), channel_id=1, replica_groups=mesh['blocks'=8,'filt'=4] {'filt'}, dimensions={0}, use_global_device_ids=true | all-gather | bytes 983040 | tf_op jit(solution)/shard_map/all_gather | solution.py:84
  49.4 1.0 fusion.254
  50.9 3.1 %pad_slice_fusion.22 = (bf16[64,4,8,128]{3,0,2,1:T(8,128)(2,1)S(1)}, bf16[64,4,8,128]{3,0,2,1:T(8,128)(2,1)S(1)}, bf16[64,4,8,128]{3,0,2,1:T(8,128)(2,1)S(1)}, b...) fusion(bf16[64,4,12,128]{3,0,2,1:T(8,128)(2,1)S(1)} %all_gather.3), kind=kLoop, calls=%fused_computation.22 | loop fusion | bytes 10747904 | tf_op jit(solution)/shard_map/slice | solution.py:27
  67.2 1.1 multiply_convert_fusion
  68.2 4.6 %collective-permute-start.4 = (bf16[16,4,1,128]{3,0,2,1:T(8,128)(2,1)S(1)}, bf16[16,4,1,128]{3,0,2,1:T(8,128)(2,1)S(1)}, u32[]{:S(2)}, u32[]{:S(2)}) collective-permute-start(bf16[16,4,1,128]{3,0,2,1:T(8,128)(2,1)S(1)} %get-tuple-element.43), channel_id=1, source_target_pairs={{0,4},{4,8},{8,12},{12,16},{16,20},{20,24},{24,28},{1,5},{5,9},{9,... | collective-permute-start | bytes 49160 | tf_op jit(solution)/shard_map/ppermute | solution.py:14
  72.8 1.5 collective-permute-start.5
  75.0 4.0 %collective-permute-done.5 = bf16[16,4,1,128]{3,0,2,1:T(8,128)(2,1)S(1)} collective-permute-done((bf16[16,4,1,128]{3,0,2,1:T(8,128)(2,1)S(1)}, bf16[16,4,1,128]{3,0,2,1:T(8,128)(2,1)S(1)}, u32[]{:S(2)}, u32[]{:S(2)}) %collective-permute-start.5) | collective-permute-done | bytes 16416 | tf_op jit(solution)/shard_map/ppermute | solution.py:17
  82.1 1.2 fusion.22
  83.3 1.3 convolution_bitcast_fusion.28
  85.7 2.2 %pad_slice_fusion.29 = (bf16[64,4,8,128]{3,0,2,1:T(8,128)(2,1)}, bf16[64,4,8,128]{3,0,2,1:T(8,128)(2,1)}, bf16[64,4,8,128]{3,0,2,1:T(8,128)(2,1)}, bf16[64,4,8,1...) fusion(bf16[64,4,14,128]{3,0,2,1:T(8,128)(2,1)S(1)} %constant_dynamic-update-slice_fusion), kind=kLoop, calls=%fused_computation.29 | loop fusion | bytes 4063232 | tf_op jit(solution)/shard_map/slice | solution.py:48
  88.3 1.3 convolution_bitcast_fusion.58
  91.0 1.1 convolution_bitcast_fusion.51
  92.1 1.1 convolution_bitcast_fusion.57
  93.2 37.6 %psum.14 = f32[3,3,16,64]{3,2,1,0:T(8,128)} all-reduce(f32[3,3,16,64]{3,2,1,0:T(8,128)S(1)} %maximum_multiply_fusion.1), channel_id=1, replica_groups=mesh['blocks'=8,'filt'=4] {'blocks'}, use_global_device_ids=true, to_apply=%region_2.3 | all-reduce | flops 9216 | bytes 73728 | tf_op jit(solution)/shard_map/psum | solution.py:103
  130.8 1.6 copy.92
  132.4 26.5 %all-reduce.6.cloned.1.call-done = f32[3,3,3,16,64]{4,3,2,1,0:T(8,128)} async-done(((f32[3,3,3,16,64]{4,3,2,1,0:T(8,128)}), f32[3,3,3,16,64]{4,3,2,1,0:T(8,128)}) %all-reduce.6.cloned.1.call-update) | async-done | bytes 110608 | tf_op jit(solution)/shard_map/psum | solution.py:103
  158.9 1.6 copy.355
  (158 shorter events, 35.5 us)
Async XLA Ops:
  8.0 59.2 %reduce-scatter.3.cloned.1.call-start = ((), (), s32[]{:S(2)}) async-start(), calls=%async_computation.2 | async-start | bytes 1310720 | tf_op jit(solution)/shard_map/reduce_scatter | solution.py:93
  9.0 14.7 %copy-start.7 = (bf16[3,3,16,64]{3,2,1,0:T(8,128)(2,1)S(1)}, bf16[3,3,16,64]{3,2,1,0:T(8,128)(2,1)}, u32[]{:S(2)}) copy-start(bf16[3,3,16,64]{3,2,1,0:T(8,128)(2,1)} %param.5) | copy-start | bytes 55300
  9.0 14.7 %copy-start.6 = (bf16[3,3,3,16,64]{4,3,2,1,0:T(8,128)(2,1)S(1)}, bf16[3,3,3,16,64]{4,3,2,1,0:T(8,128)(2,1)}, u32[]{:S(2)}) copy-start(bf16[3,3,3,16,64]{4,3,2,1,0:T(8,128)(2,1)} %param.6) | copy-start | bytes 165892
  9.0 15.3 %collective-permute-start.2 = (bf16[16,4,2,128]{3,0,2,1:T(8,128)(2,1)S(1)}, bf16[16,4,2,128]{3,0,2,1:T(8,128)(2,1)S(1)}, u32[]{:S(2)}, u32[]{:S(2)}) collective-permute-start(bf16[16,4,2,128]{3,0,2,1:T(8,128)(2,1)S(1)} %get-tuple-element.45), channel_id=1, source_target_pairs={{0,4},{4,8},{8,12},{12,16},{16,20},{20,24},{24,28},{1,5},{5,9},{9,... | collective-permute-start | bytes 98312 | tf_op jit(solution)/shard_map/ppermute | solution.py:14
  14.1 9.7 %copy-start.1 = (bf16[16,4,8,128]{3,2,1,0:T(8,128)(2,1)S(1)}, bf16[16,4,8,128]{3,2,1,0:T(8,128)(2,1)}, u32[]{:S(2)}) copy-start(bf16[16,4,8,128]{3,2,1,0:T(8,128)(2,1)} %param.7) | copy-start | bytes 393220
  14.1 10.3 %collective-permute-start.3 = (bf16[16,4,2,128]{3,0,2,1:T(8,128)(2,1)S(1)}, bf16[16,4,2,128]{3,0,2,1:T(8,128)(2,1)S(1)}, u32[]{:S(2)}, u32[]{:S(2)}) collective-permute-start(bf16[16,4,2,128]{3,0,2,1:T(8,128)(2,1)S(1)} %get-tuple-element.46), channel_id=1, source_target_pairs={{4,0},{8,4},{12,8},{16,12},{20,16},{24,20},{28,24},{5,1},{9,5},{13... | collective-permute-start | bytes 98312 | tf_op jit(solution)/shard_map/ppermute | solution.py:17
  17.0 7.1 %copy-start = (bf16[64,4,8,128]{3,2,1,0:T(8,128)(2,1)S(1)}, bf16[64,4,8,128]{3,2,1,0:T(8,128)(2,1)}, u32[]{:S(2)}) copy-start(bf16[64,4,8,128]{3,2,1,0:T(8,128)(2,1)} %param.4) | copy-start | bytes 1572868
  17.0 18.3 %collective-permute-start = (bf16[64,4,3,128]{3,0,2,1:T(8,128)(2,1)S(1)}, bf16[64,4,3,128]{3,0,2,1:T(8,128)(2,1)}, u32[]{:S(2)}, u32[]{:S(2)}) collective-permute-start(bf16[64,4,3,128]{3,0,2,1:T(8,128)(2,1)S(1)} %copy.344), channel_id=1, source_target_pairs={{0,4},{4,8},{8,12},{12,16},{16,20},{20,24},{24,28},{1,5},{5,9},{9,... | collective-permute-start | bytes 589832 | tf_op jit(solution)/shard_map/ppermute | solution.py:14
  22.4 14.1 %collective-permute-start.1 = (bf16[64,4,3,128]{3,0,2,1:T(8,128)(2,1)S(1)}, bf16[64,4,3,128]{3,0,2,1:T(8,128)(2,1)}, u32[]{:S(2)}, u32[]{:S(2)}) collective-permute-start(bf16[64,4,3,128]{3,0,2,1:T(8,128)(2,1)S(1)} %copy.345), channel_id=1, source_target_pairs={{4,0},{8,4},{12,8},{16,12},{20,16},{24,20},{28,24},{5,1},{9,5},{13... | collective-permute-start | bytes 589832 | tf_op jit(solution)/shard_map/ppermute | solution.py:17
  35.3 95.5 %reduce-scatter.5.cloned.1.call-start = ((), (), s32[]{:S(2)}) async-start(), calls=%async_computation.3 | async-start | bytes 655360 | tf_op jit(solution)/shard_map/reduce_scatter | solution.py:99
  68.2 6.8 %collective-permute-start.4 = (bf16[16,4,1,128]{3,0,2,1:T(8,128)(2,1)S(1)}, bf16[16,4,1,128]{3,0,2,1:T(8,128)(2,1)S(1)}, u32[]{:S(2)}, u32[]{:S(2)}) collective-permute-start(bf16[16,4,1,128]{3,0,2,1:T(8,128)(2,1)S(1)} %get-tuple-element.43), channel_id=1, source_target_pairs={{0,4},{4,8},{8,12},{12,16},{16,20},{20,24},{24,28},{1,5},{5,9},{9,... | collective-permute-start | bytes 49160 | tf_op jit(solution)/shard_map/ppermute | solution.py:14
  72.8 6.2 %collective-permute-start.5 = (bf16[16,4,1,128]{3,0,2,1:T(8,128)(2,1)S(1)}, bf16[16,4,1,128]{3,0,2,1:T(8,128)(2,1)S(1)}, u32[]{:S(2)}, u32[]{:S(2)}) collective-permute-start(bf16[16,4,1,128]{3,0,2,1:T(8,128)(2,1)S(1)} %get-tuple-element.44), channel_id=1, source_target_pairs={{4,0},{8,4},{12,8},{16,12},{20,16},{24,20},{28,24},{5,1},{9,5},{13... | collective-permute-start | bytes 49160 | tf_op jit(solution)/shard_map/ppermute | solution.py:17
  83.2 1.4 copy-start.5
  83.3 75.6 %all-reduce.6.cloned.1.call-start = ((), (), s32[]{:S(2)}) async-start(), calls=%async_computation.4 | async-start | bytes 442368 | tf_op jit(solution)/shard_map/psum | solution.py:103
  87.9 1.8 %copy-start.4 = (bf16[64,4,8,128]{3,0,2,1:T(8,128)(2,1)S(1)}, bf16[64,4,8,128]{3,0,2,1:T(8,128)(2,1)}, u32[]{:S(2)}) copy-start(bf16[64,4,8,128]{3,0,2,1:T(8,128)(2,1)} %get-tuple-element.9) | copy-start | bytes 1572868
  87.9 2.0 %copy-start.3 = (bf16[64,4,8,128]{3,0,2,1:T(8,128)(2,1)S(1)}, bf16[64,4,8,128]{3,0,2,1:T(8,128)(2,1)}, u32[]{:S(2)}) copy-start(bf16[64,4,8,128]{3,0,2,1:T(8,128)(2,1)} %get-tuple-element.10) | copy-start | bytes 1572868
  88.3 1.9 %copy-start.2 = (bf16[64,4,8,128]{3,0,2,1:T(8,128)(2,1)S(1)}, bf16[64,4,8,128]{3,0,2,1:T(8,128)(2,1)}, u32[]{:S(2)}) copy-start(bf16[64,4,8,128]{3,0,2,1:T(8,128)(2,1)} %get-tuple-element.11) | copy-start | bytes 1572868
Sparse Core Ops, SparseCore 0:
  35.4 27.4 reduce-scatter.2
  83.4 22.4 reduce-scatter.4
Sparse Core Ops, SparseCore 1:
  88.0 70.8 all-reduce.5
where the time goes:
time: 169 us; the launch traced here: 168 us
  blocking collectives  46.4 us (27%)
  matrix products  38.2 us (23%)
  waiting for transfers between devices  30.6 us (18%)
  starting transfers between devices  19.3 us (11%)
  between operations  16.1 us (10%)
  local copies, waits for them, and re-layouts  15.1 us (9%)
  other arithmetic  2.3 us (1%)
    psum x1, blocking collectives, per_device(): lax.psum((first_local * factor, second_local * factor), 'blocks')  37.6 us
    psum x1, waiting for transfers between devices, per_device(): lax.psum((first_local * factor, second_local * factor), 'blocks')  26.5 us
    dot_general x72, matrix products, correlate(): jnp.einsum('oi,izyx->ozyx', kernel[a, b, c], window, preferred_element_ty...  24.8 us
    ppermute x3, starting transfers between devices, extended(): lax.ppermute(lax.slice_in_dim(block, block.shape[dim] - width, None, axis...  14.9 us
    dot_general x36, matrix products, kernel_grads(): jnp.einsum('ozyx,izyx->oi', left, window, preferred_element_type=jnp.floa...  13.4 us
    all_gather x1, blocking collectives, per_device(): hidden_rim = lax.all_gather(hidden_wide, 'filt', axis=0, tiled=True)  8.77 us
    unnamed x25, local copies, waits for them, and re-layouts  6.42 us
    ppermute x3, starting transfers between devices, extended(): lax.ppermute(lax.slice_in_dim(block, 0, width, axis=dim), axis, backward)  4.23 us
  transfers between devices with their start and end apart: 9, of which 2 were waited for; matrix products, arithmetic and copies ran while one was open for 28% of the time, Pallas kernels for 0%

commit v1 on v0

v1 whole, which is shorter than its diff:
```python
import functools
import math

import jax
import jax.numpy as jnp
from jax import lax
from jax.experimental import pallas as pl
from jax.experimental.pallas import tpu as pltpu
from jax.sharding import PartitionSpec as P

HALO = 3
MESH = pl.DeviceIdType.MESH


def shifted(row, amount):
    if amount == 0:
        return row
    width = row.shape[1]
    lane = lax.broadcasted_iota(jnp.int32, row.shape, 1)
    moved = pltpu.roll(row, amount % width, 1)
    keep = lane >= amount if amount > 0 else lane < width + amount
    return jnp.where(keep, moved, 0.0)


def rows_of(ref, z, rows, width):
    pieces = []
    start = 0
    while start < len(rows):
        stop = start + 1
        while stop < len(rows) and rows[stop] == rows[stop - 1] + 1:
            stop += 1
        pieces.append(ref[z, :, rows[start] * width : (rows[stop - 1] + 1) * width])
        start = stop
    return pieces[0] if len(pieces) == 1 else jnp.concatenate(pieces, axis=1)


def taps_of(ref, z, row_lists, width):
    return jnp.concatenate([rows_of(ref, z, rows, width) for rows in row_lists], axis=0)


def gather_taps(product, width, channels, count, amounts):
    out = []
    for r in range(count):
        total = None
        for c in range(3):
            part = product[c * channels : (c + 1) * channels, r * width : (r + 1) * width]
            part = shifted(part, amounts[c])
            total = part if total is None else total + part
        out.append(total)
    return out


def dot(a, b):
    return jnp.dot(a, b, preferred_element_type=jnp.float32)


def dot_cells(a, b):
    return lax.dot_general(a, b, (((1,), (1,)), ((), ())), preferred_element_type=jnp.float32)


def kernel(
    sizes,
    vol, cot, w1p, w1g, w2g, w2o,
    out, inp, grads,
    vs, cs, hs, slope, pgs, w1f, w1t, w2f, w2t, part, landed, final, cshift,
    halo_send, halo_recv, fwd_send, fwd_recv, gat_send, gat_recv,
    rs_send, rs_recv, ag_send, ag_recv,
):
    nb, nf, y_rows, width, chunk = sizes
    z_cells, channels, _ = vol.shape
    own = cot.shape[1]
    half = channels // 2
    b = lax.axis_index("blocks")
    f = lax.axis_index("filt")
    mine = pl.ds(pl.multiple_of(f * own, own), own)
    core_half = pl.ds(pl.multiple_of(lax.rem(f, 2) * half, half), half)
    mate = f + 1 - 2 * lax.rem(f, 2)

    barrier = pltpu.get_barrier_semaphore()
    for d in range(1, nf):
        pl.semaphore_signal(barrier, 1, device_id=(b, lax.rem(f + d, nf)), device_id_type=MESH)
    for d in range(1, nb):
        pl.semaphore_signal(barrier, 1, device_id=(lax.rem(b + d, nb), f), device_id_type=MESH)
    pl.semaphore_wait(barrier, nf - 1 + nb - 1)

    hw = HALO * width
    body = y_rows * width
    low, mid, high = slice(0, hw), slice(hw, hw + body), slice(hw + body, 2 * hw + body)
    has_low, has_high = b > 0, b < nb - 1
    lands = (low, high)
    gives = (slice(body - hw, body), slice(0, hw))
    sends_if = (has_high, has_low)
    lands_if = (has_low, has_high)
    targets = (b + 1, b - 1)

    def remote(src, dst, send, recv, device):
        return pltpu.make_async_remote_copy(
            src_ref=src, dst_ref=dst, send_sem=send, recv_sem=recv, device_id=device, device_id_type=MESH
        )

    def halo(side):
        return (
            remote(vol.at[:, core_half, gives[side]], vs.at[:, core_half, lands[side]],
                   halo_send.at[side], halo_recv.at[side], (targets[side], f)),
            remote(cot.at[:, :, gives[side]], cs.at[:, mine, lands[side]],
                   halo_send.at[2 + side], halo_recv.at[2 + side], (targets[side], f)),
        )

    def forward_volume(side):
        ref = vs.at[:, core_half, lands[side]]
        return remote(ref, ref, fwd_send.at[side], fwd_recv.at[side], (b, mate))

    def forward_cot(side, d):
        ref = cs.at[:, mine, lands[side]]
        slot = 2 * d + side
        return remote(ref, ref, fwd_send.at[slot], fwd_recv.at[slot], (b, lax.rem(f + d, nf)))

    def gathers(d):
        to = lax.rem(f + d, nf)
        device = (b, to)
        pairs = (
            (w1p, w1f.at[:, mine, :]),
            (cot, cs.at[:, mine, mid]),
            (w2g, w2f.at[:, :, mine, :]),
            (w1g.at[to], w1t.at[:, mine, :]),
        )
        return [
            remote(s, t, gat_send.at[4 * d + k], gat_recv.at[4 * d + k], device)
            for k, (s, t) in enumerate(pairs)
        ]

    for side in (0, 1):
        @pl.when(sends_if[side])
        def _():
            for copy in halo(side):
                copy.start()
    gathered = [gathers(d) for d in range(1, nf)]
    for k in range(4):
        for copies in gathered:
            copies[k].start()

    vs[:, :, mid] = vol[...]
    cs[:, mine, mid] = cot[...]
    w1f[:, mine, :] = w1p[...]
    w2f[:, :, mine, :] = w2g[...]
    w1t[:, mine, :] = w1g[f]
    for side in (0, 1):
        @pl.when(jnp.logical_not(lands_if[side]))
        def _():
            vs[:, :, lands[side]] = jnp.zeros((z_cells, channels, hw), vs.dtype)
            cs[:, :, lands[side]] = jnp.zeros((z_cells, channels, hw), cs.dtype)
    for z in range(z_cells):
        for y in range(y_rows):
            at = slice(y * width, (y + 1) * width)
            row = cot[z, :, at].astype(jnp.float32)
            for c in range(3):
                cshift[z, c * own : (c + 1) * own, at] = shifted(row, 2 * (c - 1)).astype(cshift.dtype)

    for copies in gathered:
        copies[0].wait_recv()
    first_weight = w1f[...].reshape(3 * channels, w1f.shape[2])

    def first_layer(rows):
        for z in range(z_cells):
            product = dot(
                first_weight,
                taps_of(vs, z, [[y + t - 1 + HALO for y in rows] for t in range(3)], width),
            )
            for y, pre in zip(rows, gather_taps(product, width, channels, len(rows), (1, 0, -1))):
                at = slice((y + 2) * width, (y + 3) * width)
                sigma = 1.0 / (1.0 + jnp.exp(-pre))
                hs[z, :, at] = (pre * sigma).astype(hs.dtype)
                slope[z, :, at] = sigma * (1.0 + pre * (1.0 - sigma))

    inner = list(range(1, y_rows - 1))
    outer = [-2, -1, 0, y_rows - 1, y_rows, y_rows + 1]
    for k in range(0, len(inner), 2):
        first_layer(inner[k : k + 2])

    for side in (0, 1):
        @pl.when(lands_if[side])
        def _():
            volume_copy, cot_copy = halo(side)
            volume_copy.wait_recv()
            forward_volume(side).start()
            cot_copy.wait_recv()
            for d in range(1, nf):
                forward_cot(side, d).start()

    for copies in gathered:
        copies[1].wait_recv()
        copies[2].wait_recv()
    for a in range(3):
        w2t[a] = jnp.transpose(w2f[a].reshape(3 * channels, w2f.shape[3]))

    def hidden_grad(rows):
        for z in range(z_cells):
            product = None
            for a in range(3):
                at_z = z - 2 * (a - 1)
                if 0 <= at_z < z_cells:
                    term = dot(
                        w2t[a],
                        taps_of(cs, at_z, [[y - 2 * (t - 1) + HALO for y in rows] for t in range(3)], width),
                    )
                    product = term if product is None else product + term
            for y, value in zip(rows, gather_taps(product, width, channels, len(rows), (-2, 0, 2))):
                grad = value * slope[z, :, (y + 2) * width : (y + 3) * width]
                pgs[z, :, (y + 1) * width : (y + 2) * width] = grad.astype(pgs.dtype)

    inner_grad = list(range(2, y_rows - 2))
    outer_grad = [y for y in range(-1, y_rows + 1) if y not in inner_grad]
    for k in range(0, len(inner_grad), 2):
        hidden_grad(inner_grad[k : k + 2])

    for side in (0, 1):
        @pl.when(lands_if[side])
        def _():
            forward_volume(side).wait_recv()
    for k in range(0, len(outer), 2):
        first_layer(outer[k : k + 2])
    for side, at in ((0, slice(0, 2 * width)), (1, slice((y_rows + 2) * width, (y_rows + 4) * width))):
        @pl.when(jnp.logical_not(lands_if[side]))
        def _():
            hs[:, :, at] = jnp.zeros((z_cells, channels, 2 * width), hs.dtype)

    def hidden_taps(z, rows):
        return taps_of(hs, z, [[y + 2 * t for y in rows] for t in range(3)], width)

    factor = 1.0 / math.sqrt(z_cells * y_rows * nb * width)
    every = list(range(y_rows))
    for a in range(3):
        total = None
        for z in range(z_cells):
            at_z = z + 2 * (a - 1)
            if 0 <= at_z < z_cells:
                term = dot_cells(cshift[z], hidden_taps(at_z, every))
                total = term if total is None else total + term
        if total is None:
            total = jnp.zeros((3 * own, 3 * channels), jnp.float32)
        part[a * 3 * own : (a + 1) * 3 * own, :] = total * factor

    for side in (0, 1):
        @pl.when(lands_if[side])
        def _():
            for d in range(1, nf):
                forward_cot(side, d).wait_recv()
    for k in range(0, len(outer_grad), 2):
        hidden_grad(outer_grad[k : k + 2])
    for side, at in ((0, slice(0, width)), (1, slice((y_rows + 1) * width, (y_rows + 2) * width))):
        @pl.when(jnp.logical_not(lands_if[side]))
        def _():
            pgs[:, :, at] = jnp.zeros((z_cells, channels, width), pgs.dtype)

    total = None
    for z in range(z_cells):
        columns = []
        for y in range(y_rows):
            row = pgs[z, mine, (y + 1) * width : (y + 2) * width].astype(jnp.float32)
            columns.append(
                jnp.concatenate([shifted(row, c - 1).astype(pgs.dtype) for c in range(3)], axis=0)
            )
        term = dot_cells(
            jnp.concatenate(columns, axis=1),
            taps_of(vs, z, [[y + t - 1 + HALO for y in every] for t in range(3)], width),
        )
        total = term if total is None else total + term
    used = 12 * own
    part[9 * own : used, :] = total * factor
    if part.shape[0] > used:
        part[used:, :] = jnp.zeros((part.shape[0] - used, part.shape[1]), part.dtype)

    def piece(index):
        return pl.ds(pl.multiple_of(index * chunk, 8), chunk)

    scatters = []
    for d in range(1, nb):
        to = lax.rem(b + d, nb)
        copy = remote(part.at[piece(to), :], landed.at[d], rs_send.at[d], rs_recv.at[d], (to, f))
        copy.start()
        scatters.append(copy)

    for z in range(z_cells):
        for k in range(0, y_rows, 2):
            product = None
            for a in range(3):
                at_z = z + 2 * (a - 1)
                if 0 <= at_z < z_cells:
                    term = dot(w2o[a], hidden_taps(at_z, every[k : k + 2]))
                    product = term if product is None else product + term
            for y, value in zip(every[k : k + 2], gather_taps(product, width, own, 2, (2, 0, -2))):
                out[z, :, y * width : (y + 1) * width] = value.astype(out.dtype)

    total = part[piece(b), :]
    for d in range(1, nb):
        scatters[d - 1].wait_recv()
        total = total + landed[d]
    final[piece(b), :] = total
    spreads = []
    for d in range(1, nb):
        to = lax.rem(b + d, nb)
        ref = final.at[piece(b), :]
        copy = remote(ref, ref, ag_send.at[d], ag_recv.at[d], (to, f))
        copy.start()
        spreads.append(copy)

    for copies in gathered:
        copies[3].wait_recv()
    back_weight = jnp.transpose(w1t[...].reshape(3 * channels, w1t.shape[2]))
    for z in range(z_cells):
        for k in range(0, y_rows, 2):
            rows = every[k : k + 2]
            product = dot(back_weight, taps_of(pgs, z, [[y + 2 - t for y in rows] for t in range(3)], width))
            for y, value in zip(rows, gather_taps(product, width, own, 2, (-1, 0, 1))):
                inp[z, :, y * width : (y + 1) * width] = value.astype(inp.dtype)

    for copy in spreads:
        copy.wait_recv()
    grads[...] = final[:used, :]

    for side in (0, 1):
        @pl.when(sends_if[side])
        def _():
            for copy in halo(side):
                copy.wait_send()

        @pl.when(lands_if[side])
        def _():
            forward_volume(side).wait_send()
            for d in range(1, nf):
                forward_cot(side, d).wait_send()
    for copies in gathered:
        for copy in copies:
            copy.wait_send()
    for copy in scatters + spreads:
        copy.wait_send()


def per_device(nb, nf, volume, w_first, w_second, cotangent):
    channels, z_cells, y_rows, width = volume.shape
    own = cotangent.shape[0]
    cells = y_rows * width
    vol = volume.transpose(1, 0, 2, 3).reshape(z_cells, channels, cells)
    cot = cotangent.transpose(1, 0, 2, 3).reshape(z_cells, own, cells)
    w1p = w_first.transpose(1, 2, 0, 3).reshape(3, own, 3 * channels)
    w1g = w_first.reshape(3, 3, own, nf, own).transpose(3, 0, 2, 1, 4).reshape(nf, 3, own, 3 * own)
    w2g = w_second.transpose(0, 1, 3, 2, 4).reshape(3, 3, own, 3 * channels)
    w2o = w_second.transpose(0, 2, 3, 1, 4).reshape(3, 3 * own, 3 * channels)
    used = 12 * own
    chunk = -(-used // (8 * nb)) * 8
    wide = (y_rows + 2 * HALO) * width
    bf16, f32 = jnp.bfloat16, jnp.float32
    dma = pltpu.SemaphoreType.DMA
    out, inp, grads = pl.pallas_call(
        functools.partial(kernel, (nb, nf, y_rows, width, chunk)),
        out_shape=(
            jax.ShapeDtypeStruct((z_cells, own, cells), bf16),
            jax.ShapeDtypeStruct((z_cells, own, cells), bf16),
            jax.ShapeDtypeStruct((used, 3 * channels), f32),
        ),
        in_specs=[pl.BlockSpec(memory_space=pltpu.VMEM)] * 6,
        out_specs=(pl.BlockSpec(memory_space=pltpu.VMEM),) * 3,
        scratch_shapes=[
            pltpu.VMEM((z_cells, channels, wide), bf16),
            pltpu.VMEM((z_cells, channels, wide), bf16),
            pltpu.VMEM((z_cells, channels, (y_rows + 4) * width), bf16),
            pltpu.VMEM((z_cells, channels, (y_rows + 4) * width), f32),
            pltpu.VMEM((z_cells, channels, (y_rows + 2) * width), bf16),
            pltpu.VMEM((3, channels, 3 * channels), bf16),
            pltpu.VMEM((3, channels, 3 * own), bf16),
            pltpu.VMEM((3, 3, channels, 3 * channels), bf16),
            pltpu.VMEM((3, 3 * channels, 3 * channels), bf16),
            pltpu.VMEM((nb * chunk, 3 * channels), f32),
            pltpu.VMEM((nb, chunk, 3 * channels), f32),
            pltpu.VMEM((nb * chunk, 3 * channels), f32),
            pltpu.VMEM((z_cells, 3 * own, cells), bf16),
            dma((4,)), dma((4,)),
            dma((2 * nf,)), dma((2 * nf,)),
            dma((4 * nf,)), dma((4 * nf,)),
            dma((nb,)), dma((nb,)), dma((nb,)), dma((nb,)),
        ],
        compiler_params=pltpu.CompilerParams(
            collective_id=0, has_side_effects=True, vmem_limit_bytes=40 * 1024 * 1024
        ),
    )(vol, cot, w1p, w1g, w2g, w2o)
    output = out.reshape(z_cells, own, y_rows, width).transpose(1, 0, 2, 3)
    input_grad = inp.reshape(z_cells, own, y_rows, width).transpose(1, 0, 2, 3)
    second = grads[: 9 * own].reshape(3, 3, own, 3, channels).transpose(0, 3, 1, 2, 4)
    first = grads[9 * own :].reshape(3, own, 3, channels).transpose(2, 0, 1, 3)
    return (output, input_grad, first, second)


def solution(mesh):
    return jax.shard_map(
        functools.partial(per_device, mesh.shape["blocks"], mesh.shape["filt"]),
        mesh=mesh,
        in_specs=(
            P(None, None, "blocks", None),
            P(None, None, "filt", None),
            P(None, None, None, "filt", None),
            P("filt", None, "blocks", None),
        ),
        out_specs=(
            P("filt", None, "blocks", None),
            P("filt", None, "blocks", None),
            P(None, None, "filt", None),
            P(None, None, None, "filt", None),
        ),
        check_vma=False,
    )
```

time: 169 us -> 43.8 us (0.26)
  blocking collectives: 46.4 us -> 0 us
  matrix products: 38.2 us -> 0 us
  Pallas kernels: 0 us -> 35.9 us
  waiting for transfers between devices: 30.6 us -> 0 us
  starting transfers between devices: 19.3 us -> 0 us
  between operations: 16.1 us -> 0.76 us
  local copies, waits for them, and re-layouts: 15.1 us -> 6.87 us
  other arithmetic: 2.3 us -> 0 us
    dot_general x108 -> x0, matrix products: 38.2 us -> none  [the longest x72 24.8 us: correlate(): jnp.einsum('oi,izyx->ozyx', kernel[a, b, c], window, preferred_element_ty...]
    psum x1 -> x0, blocking collectives: 37.6 us -> none  [per_device(): lax.psum((first_local * factor, second_local * factor), 'blocks')]
    pallas_call x0 -> x1, Pallas kernels: none -> 35.9 us  [per_device(): pl.pallas_call(functools.partial(kernel, (nb, nf, y_rows, width, chunk)),...]
    psum x1 -> x0, waiting for transfers between devices: 26.5 us -> none  [per_device(): lax.psum((first_local * factor, second_local * factor), 'blocks')]
    ppermute x6 -> x0, starting transfers between devices: 19.2 us -> none  [the longest x3 14.9 us: extended(): lax.ppermute(lax.slice_in_dim(block, block.shape[dim] - width, None, axis...]
    all_gather x1 -> x0, blocking collectives: 8.77 us -> none  [per_device(): hidden_rim = lax.all_gather(hidden_wide, 'filt', axis=0, tiled=True)]
    slice x6 -> x2, local copies, waits for them, and re-layouts: 7.7 us -> 0.01 us  [the longest x1 0.01 us: per_device(): grads[:9 * own].reshape(3, 3, own, 3, channels).transpose(0, 3, 1, 2, 4)]
    ppermute x6 -> x0, waiting for transfers between devices: 4.03 us -> none  [the longest x3 4.02 us: extended(): lax.ppermute(lax.slice_in_dim(block, 0, width, axis=dim), axis, backward)]
  transfers between devices with their start and end apart: 9 -> 0, of which waited for: 2 -> 0; matrix products, arithmetic and copies ran while one was open for 28% -> 0% of each run, Pallas kernels for 0% -> 0%
where the time goes in v1:
time: 43.8 us; the launch traced here: 43.5 us
  Pallas kernels  35.9 us (82%)
  local copies, waits for them, and re-layouts  6.87 us (16%)
  between operations  0.76 us (2%)
    pallas_call x1, Pallas kernels, per_device(): pl.pallas_call(functools.partial(kernel, (nb, nf, y_rows, width, chunk)),...  35.9 us
    unnamed x10, local copies, waits for them, and re-layouts  3.58 us
    reshape x2, local copies, waits for them, and re-layouts, per_device(): vol = volume.transpose(1, 0, 2, 3).reshape(z_cells, channels, cells)  1.32 us

profile of v1, /device:TPU:0, one launch (start us, length us, event | category | flops | bytes accessed | tf_op | source)
XLA Modules:
  0.0 43.5 jit_solution(13631990847272316870)
XLA Ops:
  0.6 1.2 %reshape.52 = bf16[4,64,1024]{2,0,1:T(4,128)(2,1)S(1)} reshape(bf16[4,64,8,128]{3,2,0,1:T(8,128)(2,1)} %bitcast.44) | data formatting | bytes 1048576 | tf_op jit(solution)/shard_map/reshape | solution.py:343
  1.8 0.0 copy-start.1
  1.8 0.2 copy.28.vol
  2.0 0.6 %copy-done.1 = bf16[3,3,16,64]{3,2,1,0:T(8,128)(2,1)S(1)} copy-done((bf16[3,3,16,64]{3,2,1,0:T(8,128)(2,1)S(1)}, bf16[3,3,16,64]{3,2,1,0:T(8,128)(2,1)}, u32[]{:S(2)}) %copy-start.1) | copy-done | bytes 18456
  2.6 0.1 reshape.44
  2.7 0.1 copy.35
  2.8 0.0 copy-start.2
  2.8 0.1 reshape.45.w1g
  3.0 0.8 %copy-done.2 = bf16[16,4,8,128]{3,2,1,0:T(8,128)(2,1)S(1)} copy-done((bf16[16,4,8,128]{3,2,1,0:T(8,128)(2,1)S(1)}, bf16[16,4,8,128]{3,2,1,0:T(8,128)(2,1)}, u32[]{:S(2)}) %copy-start.2) | copy-done | bytes 131096
  3.8 0.0 copy-start
  3.8 0.8 %copy-done = bf16[3,3,3,16,64]{4,3,2,1,0:T(8,128)(2,1)S(1)} copy-done((bf16[3,3,3,16,64]{4,3,2,1,0:T(8,128)(2,1)S(1)}, bf16[3,3,3,16,64]{4,3,2,1,0:T(8,128)(2,1)}, u32[]{:S(2)}) %copy-start) | copy-done | bytes 55320
  4.7 0.1 copy.22
  4.7 0.1 reshape.46.w2g
  4.9 0.1 copy.23
  4.9 0.1 reshape.47.w2o
  5.1 0.1 reshape.43.w1p
  5.2 35.9 %shard_map.75 = (bf16[4,16,1024]{2,1,0:T(8,128)(2,1)S(1)}, bf16[4,16,1024]{2,1,0:T(8,128)(2,1)S(1)}, f32[192,192]{1,0:T(8,128)S(1)}) custom-call(bf16[4,64,1024]{2,1,0:T(8,128)(2,1)S(1)} %copy.28.vol, bf16[4,16,1024]{2,1,0:T(8,128)(2,1)S(1)} %copy.29.cot, bf16[3,16,192]{2,1,0:T(8,128)(2,1)S(1)} %reshape.43.w1p, bf16[4,3,16,48]{3,2,1,0:T(8,128)(2,1)S(1)} %reshape.45.w1g, ...), custom_call_target="tpu_custom_call" | custom-call | tf_op jit(solution)/shard_map/pallas_call | solution.py:354
  41.2 0.7 %copy_bitcast_fusion.1 = (bf16[16,4,8,128]{3,2,1,0:T(8,128)(2,1)}, bf16[16,4,8,128]{3,2,1,0:T(8,128)(2,1)}) fusion(bf16[4,16,8,128]{3,2,1,0:T(8,128)(2,1)S(1)} %bitcast.45, bf16[4,16,8,128]{3,2,1,0:T(8,128)(2,1)S(1)} %bitcast.46), kind=kLoop, calls=%fused_computation.1 | loop fusion | bytes 524288 | tf_op jit(solution)/shard_map/transpose | solution.py:387
  41.9 0.1 reshape.51
  42.1 0.7 %copy.27 = f32[3,3,3,16,64]{4,3,2,1,0:T(8,128)} copy(f32[3,3,3,16,64]{4,1,3,2,0:T(4,128)S(1)} %bitcast.42) | data formatting | bytes 221184
  42.8 0.1 reshape.50
  42.9 0.6 %copy.26 = f32[3,3,16,64]{3,2,1,0:T(8,128)} copy(f32[3,3,16,64]{3,0,2,1:T(4,128)S(1)} %bitcast.49) | data formatting | bytes 73728
  (7 shorter events, 0.2 us)
Async XLA Ops:
  1.8 0.8 %copy-start.1 = (bf16[3,3,16,64]{3,2,1,0:T(8,128)(2,1)S(1)}, bf16[3,3,16,64]{3,2,1,0:T(8,128)(2,1)}, u32[]{:S(2)}) copy-start(bf16[3,3,16,64]{3,2,1,0:T(8,128)(2,1)} %param.5) | copy-start | bytes 55300
  2.8 0.9 %copy-start.2 = (bf16[16,4,8,128]{3,2,1,0:T(8,128)(2,1)S(1)}, bf16[16,4,8,128]{3,2,1,0:T(8,128)(2,1)}, u32[]{:S(2)}) copy-start(bf16[16,4,8,128]{3,2,1,0:T(8,128)(2,1)} %param.7) | copy-start | bytes 393220
  3.8 0.9 %copy-start = (bf16[3,3,3,16,64]{4,3,2,1,0:T(8,128)(2,1)S(1)}, bf16[3,3,3,16,64]{4,3,2,1,0:T(8,128)(2,1)}, u32[]{:S(2)}) copy-start(bf16[3,3,3,16,64]{4,3,2,1,0:T(8,128)(2,1)} %param.6) | copy-start | bytes 165892

commit v2 on v1

--- a/solution.py
+++ b/solution.py
@@ -58,15 +58,34 @@
     return lax.dot_general(a, b, (((1,), (1,)), ((), ())), preferred_element_type=jnp.float32)
 
 
+def packed(blocks, lanes):
+    tiles = [block[:, :lanes] for block in blocks]
+    last = [block[:, lanes:] for block in blocks]
+    if len(last) % 2:
+        last.append(jnp.zeros_like(last[0]))
+    tiles += [jnp.concatenate(last[k : k + 2], axis=1) for k in range(0, len(last), 2)]
+    return tiles
+
+
+def unpacked(tiles, count, channels, index, tap):
+    if tap < 2:
+        tile = tiles[index]
+        return tile[:, tap * channels : (tap + 1) * channels]
+    tile = tiles[count + index // 2]
+    side = index % 2
+    return tile[:, side * channels : (side + 1) * channels]
+
+
 def kernel(
     sizes,
-    vol, cot, w1p, w1g, w2g, w2o,
-    out, inp, grads,
-    vs, cs, hs, slope, pgs, w1f, w1t, w2f, w2t, part, landed, final, cshift,
-    halo_send, halo_recv, fwd_send, fwd_recv, gat_send, gat_recv,
+    vol, cot, w1p, w2g, w2o,
+    out, inp, first_out, second_out,
+    vs, cs, hs, slope, pgs, w1f, w1t, w2f, w2t, cshift,
+    part1, landed1, final1, part2, landed2, final2,
+    halo_send, halo_recv, fwd_send, fwd_recv, vfwd_send, vfwd_recv, gat_send, gat_recv,
     rs_send, rs_recv, ag_send, ag_recv,
 ):
-    nb, nf, y_rows, width, chunk = sizes
+    nb, nf, y_rows, width = sizes
     z_cells, channels, _ = vol.shape
     own = cot.shape[1]
     half = channels // 2
@@ -75,6 +94,8 @@
     mine = pl.ds(pl.multiple_of(f * own, own), own)
     core_half = pl.ds(pl.multiple_of(lax.rem(f, 2) * half, half), half)
     mate = f + 1 - 2 * lax.rem(f, 2)
+    across = lax.rem(f + 2, nf)
+    theirs = pl.ds(pl.multiple_of(across * own, own), own)
 
     barrier = pltpu.get_barrier_semaphore()
     for d in range(1, nf):
@@ -108,42 +129,41 @@
 
     def forward_volume(side):
         ref = vs.at[:, core_half, lands[side]]
-        return remote(ref, ref, fwd_send.at[side], fwd_recv.at[side], (b, mate))
-
-    def forward_cot(side, d):
-        ref = cs.at[:, mine, lands[side]]
-        slot = 2 * d + side
-        return remote(ref, ref, fwd_send.at[slot], fwd_recv.at[slot], (b, lax.rem(f + d, nf)))
-
-    def gathers(d):
-        to = lax.rem(f + d, nf)
-        device = (b, to)
-        pairs = (
-            (w1p, w1f.at[:, mine, :]),
-            (cot, cs.at[:, mine, mid]),
-            (w2g, w2f.at[:, :, mine, :]),
-            (w1g.at[to], w1t.at[:, mine, :]),
-        )
-        return [
-            remote(s, t, gat_send.at[4 * d + k], gat_recv.at[4 * d + k], device)
-            for k, (s, t) in enumerate(pairs)
-        ]
-
+        return remote(ref, ref, vfwd_send.at[side], vfwd_recv.at[side], (b, mate))
+
+    roles = ((mate, mine), (across, mine), (mate, theirs))
+
+    def forward_cot(side, role):
+        to, block = roles[role]
+        ref = cs.at[:, block, lands[side]]
+        slot = 2 * role + side
+        return remote(ref, ref, fwd_send.at[slot], fwd_recv.at[slot], (b, to))
+
+    def gather(k, role):
+        to, block = roles[role]
+        source = (w1p, cot, w2g)[k]
+        ref = (w1f.at[:, block, :], cs.at[:, block, mid], w2f.at[:, :, block, :])[k]
+        if role == 2:
+            source = ref
+        slot = 3 * role + k
+        return remote(source, ref, gat_send.at[slot], gat_recv.at[slot], (b, to))
+
+    for role in (1, 0):
+        gather(0, role).start()
     for side in (0, 1):
         @pl.when(sends_if[side])
         def _():
-            for copy in halo(side):
-                copy.start()
-    gathered = [gathers(d) for d in range(1, nf)]
-    for k in range(4):
-        for copies in gathered:
-            copies[k].start()
+            volume_copy, cot_copy = halo(side)
+            cot_copy.start()
+            volume_copy.start()
+    for k in (1, 2):
+        for role in (1, 0):
+            gather(k, role).start()
 
     vs[:, :, mid] = vol[...]
     cs[:, mine, mid] = cot[...]
     w1f[:, mine, :] = w1p[...]
     w2f[:, :, mine, :] = w2g[...]
-    w1t[:, mine, :] = w1g[f]
     for side in (0, 1):
         @pl.when(jnp.logical_not(lands_if[side]))
         def _():
@@ -156,8 +176,16 @@
             for c in range(3):
                 cshift[z, c * own : (c + 1) * own, at] = shifted(row, 2 * (c - 1)).astype(cshift.dtype)
 
-    for copies in gathered:
-        copies[0].wait_recv()
+    def pass_on(k):
+        gather(k, 1).wait_recv()
+        gather(k, 2).start()
+
+    def complete(k):
+        gather(k, 0).wait_recv()
+        gather(k, 2).wait_recv()
+
+    pass_on(0)
+    complete(0)
     first_weight = w1f[...].reshape(3 * channels, w1f.shape[2])
 
     def first_layer(rows):
@@ -174,22 +202,31 @@
 
     inner = list(range(1, y_rows - 1))
     outer = [-2, -1, 0, y_rows - 1, y_rows, y_rows + 1]
-    for k in range(0, len(inner), 2):
-        first_layer(inner[k : k + 2])
-
+    chunks = [inner[k : k + 2] for k in range(0, len(inner), 2)]
+    first_layer(chunks[0])
+    pass_on(1)
+    for rows in chunks[1:2]:
+        first_layer(rows)
     for side in (0, 1):
         @pl.when(lands_if[side])
         def _():
             volume_copy, cot_copy = halo(side)
-            volume_copy.wait_recv()
+            cot_copy.wait_recv()
+            forward_cot(side, 1).start()
+            forward_cot(side, 0).start()
+    for rows in chunks[2:]:
+        first_layer(rows)
+    pass_on(2)
+    for side in (0, 1):
+        @pl.when(lands_if[side])
+        def _():
+            halo(side)[0].wait_recv()
             forward_volume(side).start()
-            cot_copy.wait_recv()
-            for d in range(1, nf):
-                forward_cot(side, d).start()
-
-    for copies in gathered:
-        copies[1].wait_recv()
-        copies[2].wait_recv()
+
+    for c in range(3):
+        w1t[c] = jnp.transpose(w1f[c])
+    complete(1)
+    complete(2)
     for a in range(3):
         w2t[a] = jnp.transpose(w2f[a].reshape(3 * channels, w2f.shape[3]))
 
@@ -217,6 +254,8 @@
         @pl.when(lands_if[side])
         def _():
             forward_volume(side).wait_recv()
+            forward_cot(side, 1).wait_recv()
+            forward_cot(side, 2).start()
     for k in range(0, len(outer), 2):
         first_layer(outer[k : k + 2])
     for side, at in ((0, slice(0, 2 * width)), (1, slice((y_rows + 2) * width, (y_rows + 4) * width))):
@@ -229,6 +268,57 @@
 
     factor = 1.0 / math.sqrt(z_cells * y_rows * nb * width)
     every = list(range(y_rows))
+    lanes = 2 * channels
+
+    def reduction(which, part, landed, final):
+        chunk = part.shape[0] // nb
+
+        def piece(index):
+            return pl.ds(index * chunk, chunk)
+
+        def scatter(d):
+            to = lax.rem(b + d, nb)
+            slot = which * nb + d
+            return remote(part.at[piece(to)], landed.at[d], rs_send.at[slot], rs_recv.at[slot], (to, f))
+
+        def spread(d):
+            ref = final.at[piece(b)]
+            slot = which * nb + d
+            return remote(ref, ref, ag_send.at[slot], ag_recv.at[slot], (lax.rem(b + d, nb), f))
+
+        def fill(blocks):
+            tiles = packed(blocks, lanes)
+            for k, tile in enumerate(tiles):
+                part[k] = (tile * factor).astype(part.dtype)
+            for k in range(len(tiles), part.shape[0]):
+                part[k] = jnp.zeros(part.shape[1:], part.dtype)
+            for d in range(1, nb):
+                scatter(d).start()
+
+        def turn():
+            total = part[piece(b)].astype(jnp.float32)
+            for d in range(1, nb):
+                scatter(d).wait_recv()
+                total = total + landed[d].astype(jnp.float32)
+            final[piece(b)] = total.astype(final.dtype)
+            for d in range(1, nb):
+                spread(d).start()
+
+        def finish():
+            for d in range(1, nb):
+                spread(d).wait_recv()
+
+        def drain():
+            for d in range(1, nb):
+                scatter(d).wait_send()
+                spread(d).wait_send()
+
+        return fill, turn, finish, drain
+
+    first_sum = reduction(0, part1, landed1, final1)
+    second_sum = reduction(1, part2, landed2, final2)
+
+    blocks = []
     for a in range(3):
         total = None
         for z in range(z_cells):
@@ -238,13 +328,14 @@
                 total = term if total is None else total + term
         if total is None:
             total = jnp.zeros((3 * own, 3 * channels), jnp.float32)
-        part[a * 3 * own : (a + 1) * 3 * own, :] = total * factor
+        blocks += [total[c * own : (c + 1) * own] for c in range(3)]
+    second_sum[0](blocks)
 
     for side in (0, 1):
         @pl.when(lands_if[side])
         def _():
-            for d in range(1, nf):
-                forward_cot(side, d).wait_recv()
+            forward_cot(side, 0).wait_recv()
+            forward_cot(side, 2).wait_recv()
     for k in range(0, len(outer_grad), 2):
         hidden_grad(outer_grad[k : k + 2])
     for side, at in ((0, slice(0, width)), (1, slice((y_rows + 1) * width, (y_rows + 2) * width))):
@@ -265,20 +356,8 @@
             taps_of(vs, z, [[y + t - 1 + HALO for y in every] for t in range(3)], width),
         )
         total = term if total is None else total + term
-    used = 12 * own
-    part[9 * own : used, :] = total * factor
-    if part.shape[0] > used:
-        part[used:, :] = jnp.zeros((part.shape[0] - used, part.shape[1]), part.dtype)
-
-    def piece(index):
-        return pl.ds(pl.multiple_of(index * chunk, 8), chunk)
-
-    scatters = []
-    for d in range(1, nb):
-        to = lax.rem(b + d, nb)
-        copy = remote(part.at[piece(to), :], landed.at[d], rs_send.at[d], rs_recv.at[d], (to, f))
-        copy.start()
-        scatters.append(copy)
+    first_sum[0]([total[c * own : (c + 1) * own] for c in range(3)])
+    second_sum[1]()
 
     for z in range(z_cells):
         for k in range(0, y_rows, 2):
@@ -291,22 +370,17 @@
             for y, value in zip(every[k : k + 2], gather_taps(product, width, own, 2, (2, 0, -2))):
                 out[z, :, y * width : (y + 1) * width] = value.astype(out.dtype)
 
-    total = part[piece(b), :]
-    for d in range(1, nb):
-        scatters[d - 1].wait_recv()
-        total = total + landed[d]
-    final[piece(b), :] = total
-    spreads = []
-    for d in range(1, nb):
-        to = lax.rem(b + d, nb)
-        ref = final.at[piece(b), :]
-        copy = remote(ref, ref, ag_send.at[d], ag_recv.at[d], (to, f))
-        copy.start()
-        spreads.append(copy)
-
-    for copies in gathered:
-        copies[3].wait_recv()
-    back_weight = jnp.transpose(w1t[...].reshape(3 * channels, w1t.shape[2]))
+    first_sum[1]()
+
+    back_weight = jnp.concatenate(
+        [
+            jnp.concatenate(
+                [w1t[c, pl.ds(pl.multiple_of(t * channels + f * own, own), own), :] for t in range(3)], axis=1
+            )
+            for c in range(3)
+        ],
+        axis=0,
+    )
     for z in range(z_cells):
         for k in range(0, y_rows, 2):
             rows = every[k : k + 2]
@@ -314,9 +388,17 @@
             for y, value in zip(rows, gather_taps(product, width, own, 2, (-1, 0, 1))):
                 inp[z, :, y * width : (y + 1) * width] = value.astype(inp.dtype)
 
-    for copy in spreads:
-        copy.wait_recv()
-    grads[...] = final[:used, :]
+    second_sum[2]()
+    tiles = [final2[k].astype(jnp.float32) for k in range(14)]
+    for a in range(3):
+        for t in range(3):
+            for c in range(3):
+                second_out[a, t, c] = unpacked(tiles, 9, channels, 3 * a + c, t)
+    first_sum[2]()
+    tiles = [final1[k].astype(jnp.float32) for k in range(5)]
+    for t in range(3):
+        for c in range(3):
+            first_out[t, c] = unpacked(tiles, 3, channels, c, t)
 
     for side in (0, 1):
         @pl.when(sends_if[side])
@@ -327,13 +409,13 @@
         @pl.when(lands_if[side])
         def _():
             forward_volume(side).wait_send()
-            for d in range(1, nf):
-                forward_cot(side, d).wait_send()
-    for copies in gathered:
-        for copy in copies:
-            copy.wait_send()
-    for copy in scatters + spreads:
-        copy.wait_send()
+            for role in range(3):
+                forward_cot(side, role).wait_send()
+    for role in range(3):
+        for k in range(3):
+            gather(k, role).wait_send()
+    first_sum[3]()
+    second_sum[3]()
 
 
 def per_device(nb, nf, volume, w_first, w_second, cotangent):
@@ -343,23 +425,23 @@
     vol = volume.transpose(1, 0, 2, 3).reshape(z_cells, channels, cells)
     cot = cotangent.transpose(1, 0, 2, 3).reshape(z_cells, own, cells)
     w1p = w_first.transpose(1, 2, 0, 3).reshape(3, own, 3 * channels)
-    w1g = w_first.reshape(3, 3, own, nf, own).transpose(3, 0, 2, 1, 4).reshape(nf, 3, own, 3 * own)
     w2g = w_second.transpose(0, 1, 3, 2, 4).reshape(3, 3, own, 3 * channels)
     w2o = w_second.transpose(0, 2, 3, 1, 4).reshape(3, 3 * own, 3 * channels)
-    used = 12 * own
-    chunk = -(-used // (8 * nb)) * 8
+    tiles1, tiles2 = (-(-count // nb) * nb for count in (5, 14))
+    tile = (own, 2 * channels)
     wide = (y_rows + 2 * HALO) * width
     bf16, f32 = jnp.bfloat16, jnp.float32
     dma = pltpu.SemaphoreType.DMA
-    out, inp, grads = pl.pallas_call(
-        functools.partial(kernel, (nb, nf, y_rows, width, chunk)),
+    out, inp, first, second = pl.pallas_call(
+        functools.partial(kernel, (nb, nf, y_rows, width)),
         out_shape=(
             jax.ShapeDtypeStruct((z_cells, own, cells), bf16),
             jax.ShapeDtypeStruct((z_cells, own, cells), bf16),
-            jax.ShapeDtypeStruct((used, 3 * channels), f32),
+            jax.ShapeDtypeStruct((3, 3, own, channels), f32),
+            jax.ShapeDtypeStruct((3, 3, 3, own, channels), f32),
         ),
-        in_specs=[pl.BlockSpec(memory_space=pltpu.VMEM)] * 6,
-        out_specs=(pl.BlockSpec(memory_space=pltpu.VMEM),) * 3,
+        in_specs=[pl.BlockSpec(memory_space=pltpu.VMEM)] * 5,
+        out_specs=(pl.BlockSpec(memory_space=pltpu.VMEM),) * 4,
         scratch_shapes=[
             pltpu.VMEM((z_cells, channels, wide), bf16),
             pltpu.VMEM((z_cells, channels, wide), bf16),
@@ -367,26 +449,25 @@
             pltpu.VMEM((z_cells, channels, (y_rows + 4) * width), f32),
             pltpu.VMEM((z_cells, channels, (y_rows + 2) * width), bf16),
             pltpu.VMEM((3, channels, 3 * channels), bf16),
-            pltpu.VMEM((3, channels, 3 * own), bf16),
+            pltpu.VMEM((3, 3 * channels, channels), bf16),
             pltpu.VMEM((3, 3, channels, 3 * channels), bf16),
             pltpu.VMEM((3, 3 * channels, 3 * channels), bf16),
-            pltpu.VMEM((nb * chunk, 3 * channels), f32),
-            pltpu.VMEM((nb, chunk, 3 * channels), f32),
-            pltpu.VMEM((nb * chunk, 3 * channels), f32),
             pltpu.VMEM((z_cells, 3 * own, cells), bf16),
-            dma((4,)), dma((4,)),
-            dma((2 * nf,)), dma((2 * nf,)),
-            dma((4 * nf,)), dma((4 * nf,)),
-            dma((nb,)), dma((nb,)), dma((nb,)), dma((nb,)),
+            pltpu.VMEM((tiles1,) + tile, bf16),
+            pltpu.VMEM((nb, tiles1 // nb) + tile, bf16),
+            pltpu.VMEM((tiles1,) + tile, bf16),
+            pltpu.VMEM((tiles2,) + tile, bf16),
+            pltpu.VMEM((nb, tiles2 // nb) + tile, bf16),
+            pltpu.VMEM((tiles2,) + tile, bf16),
+            dma((4,)), dma((4,)), dma((6,)), dma((6,)), dma((2,)), dma((2,)), dma((9,)), dma((9,)),
+            dma((2 * nb,)), dma((2 * nb,)), dma((2 * nb,)), dma((2 * nb,)),
         ],
         compiler_params=pltpu.CompilerParams(
             collective_id=0, has_side_effects=True, vmem_limit_bytes=40 * 1024 * 1024
         ),
-    )(vol, cot, w1p, w1g, w2g, w2o)
+    )(vol, cot, w1p, w2g, w2o)
     output = out.reshape(z_cells, own, y_rows, width).transpose(1, 0, 2, 3)
     input_grad = inp.reshape(z_cells, own, y_rows, width).transpose(1, 0, 2, 3)
-    second = grads[: 9 * own].reshape(3, 3, own, 3, channels).transpose(0, 3, 1, 2, 4)
-    first = grads[9 * own :].reshape(3, own, 3, channels).transpose(2, 0, 1, 3)
     return (output, input_grad, first, second)
 
 

time: 43.8 us -> 34.8 us (0.79)
  Pallas kernels: 35.9 us -> 28.6 us
  local copies, waits for them, and re-layouts: 6.87 us -> 5.26 us
    pallas_call x1, Pallas kernels: 35.9 us -> 28.6 us  [per_device(): pl.pallas_call(functools.partial(kernel, (nb, nf, y_rows, width)), out_sh...]
    reshape x2, local copies, waits for them, and re-layouts: 1.32 us -> 0.28 us  [per_device(): vol = volume.transpose(1, 0, 2, 3).reshape(z_cells, channels, cells)]
    transpose x1, local copies, waits for them, and re-layouts: 0.02 us -> 0.82 us  [per_device(): w1p = w_first.transpose(1, 2, 0, 3).reshape(3, own, 3 * channels)]
    unnamed x10, local copies, waits for them, and re-layouts: 3.58 us -> 2.83 us
    reshape x5 -> x0, local copies, waits for them, and re-layouts: 0.61 us -> none  [the longest x3 0.38 us: per_device(): w_first.reshape(3, 3, own, nf, own).transpose(3, 0, 2, 1, 4)]
where the time goes in v2:
time: 34.8 us; the launch traced here: 34.6 us
  Pallas kernels  28.6 us (82%)
  local copies, waits for them, and re-layouts  5.26 us (15%)
  between operations  0.72 us (2%)
    pallas_call x1, Pallas kernels, per_device(): pl.pallas_call(functools.partial(kernel, (nb, nf, y_rows, width)), out_sh...  28.6 us
    unnamed x10, local copies, waits for them, and re-layouts  2.83 us
    transpose x1, local copies, waits for them, and re-layouts, per_device(): w1p = w_first.transpose(1, 2, 0, 3).reshape(3, own, 3 * channels)  0.82 us
    transpose x1, local copies, waits for them, and re-layouts, per_device(): input_grad = inp.reshape(z_cells, own, y_rows, width).transpose(1, 0, 2, 3)  0.75 us

profile of v2, /device:TPU:0, one launch (start us, length us, event | category | flops | bytes accessed | tf_op | source)
XLA Modules:
  0.0 34.6 jit_solution(14063935694224986806)
XLA Ops:
  0.6 0.0 copy-start.2
  0.6 0.8 %copy.17 = bf16[3,16,3,64]{3,2,1,0:T(4,128)(2,1)S(1)} copy(bf16[3,16,3,64]{3,1,0,2:T(8,128)(2,1)} %bitcast.41) | data formatting | bytes 36864 | tf_op jit(solution)/shard_map/transpose | solution.py:427
  1.5 0.1 reshape.31.w1p
  1.6 0.0 copy-done.2
  1.6 0.0 copy-start.1
  1.7 0.8 %copy-done.1 = bf16[3,3,3,16,64]{4,3,2,1,0:T(8,128)(2,1)S(1)} copy-done((bf16[3,3,3,16,64]{4,3,2,1,0:T(8,128)(2,1)S(1)}, bf16[3,3,3,16,64]{4,3,2,1,0:T(8,128)(2,1)}, u32[]{:S(2)}) %copy-start.1) | copy-done | bytes 55320
  2.5 0.0 copy-start
  2.5 0.1 copy.18
  2.6 0.1 reshape.32.w2g
  2.7 0.1 copy.19
  2.8 0.1 reshape.33.w2o
  2.9 0.6 %copy-done = bf16[64,4,8,128]{3,2,1,0:T(8,128)(2,1)S(1)} copy-done((bf16[64,4,8,128]{3,2,1,0:T(8,128)(2,1)S(1)}, bf16[64,4,8,128]{3,2,1,0:T(8,128)(2,1)}, u32[]{:S(2)}) %copy-start) | copy-done | bytes 524312
  3.6 0.1 reshape.36
  3.7 0.2 copy.22.vol
  3.8 28.6 %shard_map.75 = (bf16[4,16,1024]{2,1,0:T(8,128)(2,1)S(1)}, bf16[4,16,1024]{2,1,0:T(8,128)(2,1)S(1)}, f32[3,3,16,64]{3,2,1,0:T(8,128)S(1)}, f32[3,3,3,16,64]{4,3,2,1,0:T(8,128)S(1)}) custom-call(bf16[4,64,1024]{2,1,0:T(8,128)(2,1)S(1)} %copy.22.vol, bf16[4,16,1024]{2,1,0:T(8,128)(2,1)S(1)} %copy.23.cot, bf16[3,16,192]{2,1,0:T(8,128)(2,1)S(1)} %reshape.31.w1p, ...), custom_call_target="tpu_custom_call" | custom-call | tf_op jit(solution)/shard_map/pallas_call | solution.py:435
  32.5 0.7 %copy_bitcast_fusion = (bf16[16,4,8,128]{3,2,1,0:T(8,128)(2,1)}, bf16[16,4,8,128]{3,2,1,0:T(8,128)(2,1)}) fusion(bf16[4,16,8,128]{3,2,1,0:T(8,128)(2,1)S(1)} %bitcast.36, bf16[4,16,8,128]{3,2,1,0:T(8,128)(2,1)S(1)} %bitcast.37), kind=kLoop, calls=%fused_computation | loop fusion | bytes 524288 | tf_op jit(solution)/shard_map/transpose | solution.py:470
  33.3 0.6 %copy.30 = f32[3,3,16,64]{3,2,1,0:T(8,128)} copy(f32[3,3,16,64]{3,2,1,0:T(8,128)S(1)} %get-tuple-element.20) | data formatting | bytes 73728
  33.9 0.7 %copy.31 = f32[3,3,3,16,64]{4,3,2,1,0:T(8,128)} copy(f32[3,3,3,16,64]{4,3,2,1,0:T(8,128)S(1)} %get-tuple-element.21) | data formatting | bytes 221184
  (4 shorter events, 0.1 us)
Async XLA Ops:
  0.6 0.9 %copy-start.2 = (bf16[16,4,8,128]{3,2,1,0:T(8,128)(2,1)S(1)}, bf16[16,4,8,128]{3,2,1,0:T(8,128)(2,1)}, u32[]{:S(2)}) copy-start(bf16[16,4,8,128]{3,2,1,0:T(8,128)(2,1)} %param.7) | copy-start | bytes 393220
  1.6 0.9 %copy-start.1 = (bf16[3,3,3,16,64]{4,3,2,1,0:T(8,128)(2,1)S(1)}, bf16[3,3,3,16,64]{4,3,2,1,0:T(8,128)(2,1)}, u32[]{:S(2)}) copy-start(bf16[3,3,3,16,64]{4,3,2,1,0:T(8,128)(2,1)} %param.6) | copy-start | bytes 165892
  2.5 1.0 %copy-start = (bf16[64,4,8,128]{3,2,1,0:T(8,128)(2,1)S(1)}, bf16[64,4,8,128]{3,2,1,0:T(8,128)(2,1)}, u32[]{:S(2)}) copy-start(bf16[64,4,8,128]{3,2,1,0:T(8,128)(2,1)} %param.4) | copy-start | bytes 1572868

commit v3 on v2

--- a/solution.py
+++ b/solution.py
@@ -78,16 +78,17 @@
 
 def kernel(
     sizes,
-    vol, cot, w1p, w2g, w2o,
+    volume, w_first, w_second, cotangent,
     out, inp, first_out, second_out,
     vs, cs, hs, slope, pgs, w1f, w1t, w2f, w2t, cshift,
     part1, landed1, final1, part2, landed2, final2,
+    raw_vol, raw_cot, raw_first, raw_second, vol, cot, w1p, w2g, w2o, load_sem,
     halo_send, halo_recv, fwd_send, fwd_recv, vfwd_send, vfwd_recv, gat_send, gat_recv,
     rs_send, rs_recv, ag_send, ag_recv,
 ):
     nb, nf, y_rows, width = sizes
-    z_cells, channels, _ = vol.shape
-    own = cot.shape[1]
+    channels, z_cells = volume.shape[:2]
+    own = cotangent.shape[0]
     half = channels // 2
     b = lax.axis_index("blocks")
     f = lax.axis_index("filt")
@@ -102,7 +103,15 @@
         pl.semaphore_signal(barrier, 1, device_id=(b, lax.rem(f + d, nf)), device_id_type=MESH)
     for d in range(1, nb):
         pl.semaphore_signal(barrier, 1, device_id=(lax.rem(b + d, nb), f), device_id_type=MESH)
-    pl.semaphore_wait(barrier, nf - 1 + nb - 1)
+
+    loads = [
+        pltpu.make_async_copy(source, target, load_sem.at[k])
+        for k, (source, target) in enumerate(
+            ((cotangent, raw_cot), (w_first, raw_first), (volume, raw_vol), (w_second, raw_second))
+        )
+    ]
+    for copy in loads:
+        copy.start()
 
     hw = HALO * width
     body = y_rows * width
@@ -148,6 +157,38 @@
         slot = 3 * role + k
         return remote(source, ref, gat_send.at[slot], gat_recv.at[slot], (b, to))
 
+    def rows_first(raw, z):
+        return jnp.transpose(raw[:, z].astype(jnp.float32), (1, 0, 2)).astype(raw.dtype)
+
+    loads[0].wait()
+    for z in range(z_cells):
+        rows = rows_first(raw_cot, z)
+        for y in range(y_rows):
+            cot[z, :, y * width : (y + 1) * width] = rows[y]
+    loads[1].wait()
+    for c in range(3):
+        w1p[c] = jnp.concatenate([raw_first[t, c] for t in range(3)], axis=1)
+    loads[2].wait()
+    for z in range(z_cells):
+        rows = rows_first(raw_vol, z)
+        for y in range(y_rows):
+            vol[z, :, y * width : (y + 1) * width] = rows[y]
+    loads[3].wait()
+    for a in range(3):
+        for t in range(3):
+            w2g[a, t] = jnp.concatenate([raw_second[a, t, c] for c in range(3)], axis=1)
+        for c in range(3):
+            w2o[a, c * own : (c + 1) * own] = jnp.concatenate([raw_second[a, t, c] for t in range(3)], axis=1)
+    vs[:, :, mid] = vol[...]
+    cs[:, mine, mid] = cot[...]
+    w1f[:, mine, :] = w1p[...]
+    w2f[:, :, mine, :] = w2g[...]
+    for side in (0, 1):
+        @pl.when(jnp.logical_not(lands_if[side]))
+        def _():
+            vs[:, :, lands[side]] = jnp.zeros((z_cells, channels, hw), vs.dtype)
+            cs[:, :, lands[side]] = jnp.zeros((z_cells, channels, hw), cs.dtype)
+    pl.semaphore_wait(barrier, nf - 1 + nb - 1)
     for role in (1, 0):
         gather(0, role).start()
     for side in (0, 1):
@@ -160,15 +201,6 @@
         for role in (1, 0):
             gather(k, role).start()
 
-    vs[:, :, mid] = vol[...]
-    cs[:, mine, mid] = cot[...]
-    w1f[:, mine, :] = w1p[...]
-    w2f[:, :, mine, :] = w2g[...]
-    for side in (0, 1):
-        @pl.when(jnp.logical_not(lands_if[side]))
-        def _():
-            vs[:, :, lands[side]] = jnp.zeros((z_cells, channels, hw), vs.dtype)
-            cs[:, :, lands[side]] = jnp.zeros((z_cells, channels, hw), cs.dtype)
     for z in range(z_cells):
         for y in range(y_rows):
             at = slice(y * width, (y + 1) * width)
@@ -418,15 +450,22 @@
     second_sum[3]()
 
 
+def hand_out(out, inp, first, second, out_to, inp_to, first_to, second_to, sem):
+    z_cells = out.shape[0]
+    pairs = [(out.at[z], out_to.at[:, z]) for z in range(z_cells)]
+    pairs += [(inp.at[z], inp_to.at[:, z]) for z in range(z_cells)]
+    pairs += [(first, first_to), (second, second_to)]
+    copies = [pltpu.make_async_copy(s, t, sem.at[k]) for k, (s, t) in enumerate(pairs)]
+    for copy in copies:
+        copy.start()
+    for copy in copies:
+        copy.wait()
+
+
 def per_device(nb, nf, volume, w_first, w_second, cotangent):
     channels, z_cells, y_rows, width = volume.shape
     own = cotangent.shape[0]
     cells = y_rows * width
-    vol = volume.transpose(1, 0, 2, 3).reshape(z_cells, channels, cells)
-    cot = cotangent.transpose(1, 0, 2, 3).reshape(z_cells, own, cells)
-    w1p = w_first.transpose(1, 2, 0, 3).reshape(3, own, 3 * channels)
-    w2g = w_second.transpose(0, 1, 3, 2, 4).reshape(3, 3, own, 3 * channels)
-    w2o = w_second.transpose(0, 2, 3, 1, 4).reshape(3, 3 * own, 3 * channels)
     tiles1, tiles2 = (-(-count // nb) * nb for count in (5, 14))
     tile = (own, 2 * channels)
     wide = (y_rows + 2 * HALO) * width
@@ -440,7 +479,7 @@
             jax.ShapeDtypeStruct((3, 3, own, channels), f32),
             jax.ShapeDtypeStruct((3, 3, 3, own, channels), f32),
         ),
-        in_specs=[pl.BlockSpec(memory_space=pltpu.VMEM)] * 5,
+        in_specs=[pl.BlockSpec(memory_space=pltpu.HBM)] * 4,
         out_specs=(pl.BlockSpec(memory_space=pltpu.VMEM),) * 4,
         scratch_shapes=[
             pltpu.VMEM((z_cells, channels, wide), bf16),
@@ -459,15 +498,36 @@
             pltpu.VMEM((tiles2,) + tile, bf16),
             pltpu.VMEM((nb, tiles2 // nb) + tile, bf16),
             pltpu.VMEM((tiles2,) + tile, bf16),
+            pltpu.VMEM(volume.shape, bf16),
+            pltpu.VMEM(cotangent.shape, bf16),
+            pltpu.VMEM(w_first.shape, bf16),
+            pltpu.VMEM(w_second.shape, bf16),
+            pltpu.VMEM((z_cells, channels, cells), bf16),
+            pltpu.VMEM((z_cells, own, cells), bf16),
+            pltpu.VMEM((3, own, 3 * channels), bf16),
+            pltpu.VMEM((3, 3, own, 3 * channels), bf16),
+            pltpu.VMEM((3, 3 * own, 3 * channels), bf16),
+            dma((4,)),
             dma((4,)), dma((4,)), dma((6,)), dma((6,)), dma((2,)), dma((2,)), dma((9,)), dma((9,)),
             dma((2 * nb,)), dma((2 * nb,)), dma((2 * nb,)), dma((2 * nb,)),
         ],
         compiler_params=pltpu.CompilerParams(
             collective_id=0, has_side_effects=True, vmem_limit_bytes=40 * 1024 * 1024
         ),
-    )(vol, cot, w1p, w2g, w2o)
-    output = out.reshape(z_cells, own, y_rows, width).transpose(1, 0, 2, 3)
-    input_grad = inp.reshape(z_cells, own, y_rows, width).transpose(1, 0, 2, 3)
+    )(volume, w_first, w_second, cotangent)
+    planes = (z_cells, own, y_rows, width)
+    output, input_grad, first, second = pl.pallas_call(
+        hand_out,
+        out_shape=(
+            jax.ShapeDtypeStruct(cotangent.shape, bf16),
+            jax.ShapeDtypeStruct(cotangent.shape, bf16),
+            jax.ShapeDtypeStruct(first.shape, f32),
+            jax.ShapeDtypeStruct(second.shape, f32),
+        ),
+        in_specs=[pl.BlockSpec(memory_space=pltpu.VMEM)] * 4,
+        out_specs=(pl.BlockSpec(memory_space=pltpu.HBM),) * 4,
+        scratch_shapes=[dma((2 * z_cells + 2,))],
+    )(out.reshape(planes), inp.reshape(planes), first, second)
     return (output, input_grad, first, second)
 
 

time: 34.8 us -> 37.2 us (1.069)
  Pallas kernels: 28.6 us -> 30.6 us
  local copies, waits for them, and re-layouts: 5.26 us -> 5.64 us
    unnamed x10 -> x14, local copies, waits for them, and re-layouts: 2.83 us -> 5.64 us
    pallas_call x0 -> x1, Pallas kernels: none -> 1.98 us  [per_device(): pl.pallas_call(hand_out, out_shape=(jax.ShapeDtypeStruct(cotangent.shape,...]
    transpose x4 -> x0, local copies, waits for them, and re-layouts: 1.68 us -> none  [the longest x1 0.82 us: per_device(): w1p = w_first.transpose(1, 2, 0, 3).reshape(3, own, 3 * channels)]
    reshape x7 -> x0, local copies, waits for them, and re-layouts: 0.75 us -> none  [the longest x2 0.28 us: per_device(): vol = volume.transpose(1, 0, 2, 3).reshape(z_cells, channels, cells)]
where the time goes in v3:
time: 37.2 us; the launch traced here: 36.9 us
  Pallas kernels  30.6 us (82%)
  local copies, waits for them, and re-layouts  5.64 us (15%)
  between operations  0.66 us (2%)
    pallas_call x1, Pallas kernels, per_device(): pl.pallas_call(functools.partial(kernel, (nb, nf, y_rows, width)), out_sh...  28.6 us
    unnamed x14, local copies, waits for them, and re-layouts  5.64 us
    pallas_call x1, Pallas kernels, per_device(): pl.pallas_call(hand_out, out_shape=(jax.ShapeDtypeStruct(cotangent.shape,...  1.98 us

profile of v3, /device:TPU:0, one launch (start us, length us, event | category | flops | bytes accessed | tf_op | source)
XLA Modules:
  0.0 36.9 jit_solution(2900629842366484228)
XLA Ops:
  0.6 0.0 copy-start
  0.6 1.0 %copy-done = bf16[64,4,8,128]{3,2,1,0:T(8,128)(2,1)S(1)} copy-done((bf16[64,4,8,128]{3,2,1,0:T(8,128)(2,1)S(1)}, bf16[64,4,8,128]{3,2,1,0:T(8,128)(2,1)}, u32[]{:S(2)}) %copy-start) | copy-done | bytes 524312
  1.7 0.0 copy-start.2
  1.7 0.9 %copy-done.2 = bf16[16,4,8,128]{3,2,1,0:T(8,128)(2,1)S(1)} copy-done((bf16[16,4,8,128]{3,2,1,0:T(8,128)(2,1)S(1)}, bf16[16,4,8,128]{3,2,1,0:T(8,128)(2,1)}, u32[]{:S(2)}) %copy-start.2) | copy-done | bytes 131096
  2.6 0.0 copy-start.3
  2.6 0.9 %copy-done.3 = bf16[3,3,3,16,64]{4,3,2,1,0:T(8,128)(2,1)S(1)} copy-done((bf16[3,3,3,16,64]{4,3,2,1,0:T(8,128)(2,1)S(1)}, bf16[3,3,3,16,64]{4,3,2,1,0:T(8,128)(2,1)}, u32[]{:S(2)}) %copy-start.3) | copy-done | bytes 55320
  3.5 0.0 copy-start.5
  3.5 0.8 %copy-done.5 = bf16[3,3,16,64]{3,2,1,0:T(8,128)(2,1)S(1)} copy-done((bf16[3,3,16,64]{3,2,1,0:T(8,128)(2,1)S(1)}, bf16[3,3,16,64]{3,2,1,0:T(8,128)(2,1)}, u32[]{:S(2)}) %copy-start.5) | copy-done | bytes 18456
  4.2 28.6 %shard_map.75 = (bf16[4,16,1024]{2,1,0:T(8,128)(2,1)S(1)}, bf16[4,16,1024]{2,1,0:T(8,128)(2,1)S(1)}, f32[3,3,16,64]{3,2,1,0:T(8,128)S(1)}, f32[3,3,3,16,64]{4,3,2,1,0:T(8,128)S(1)}) custom-call(bf16[64,4,8,128]{3,2,1,0:T(8,128)(2,1)S(1)} %copy-done, bf16[3,3,16,64]{3,2,1,0:T(8,128)(2,1)S(1)} %copy-done.5, bf16[3,3,3,16,64]{4,3,2,1,0:T(8,128)(2,1)S(1)} %copy-done.3, ...), custom_call_target="tpu_custom_call" | custom-call | tf_op jit(solution)/shard_map/pallas_call | solution.py:474
  32.9 0.0 copy-start.4
  32.9 0.6 %copy-done.4 = f32[3,3,16,64]{3,2,1,0:T(8,128)} copy-done((f32[3,3,16,64]{3,2,1,0:T(8,128)}, f32[3,3,16,64]{3,2,1,0:T(8,128)S(1)}, u32[]{:S(2)}) %copy-start.4) | copy-done | bytes 36888
  33.5 0.0 copy-start.1
  33.5 0.7 %copy.8 = bf16[8,8,8,128]{3,2,1,0:T(8,128)(2,1)} copy(bf16[8,8,8,128]{3,1,2,0:T(8,128)(2,1)S(1)} %bitcast.9) | data formatting | bytes 262144
  34.2 0.7 %copy.9 = bf16[8,8,8,128]{3,2,1,0:T(8,128)(2,1)} copy(bf16[8,8,8,128]{3,1,2,0:T(8,128)(2,1)S(1)} %bitcast.8) | data formatting | bytes 262144
  34.9 0.0 copy-done.1
  34.9 2.0 %shard_map.76 = (bf16[16,4,8,128]{3,2,1,0:T(8,128)(2,1)}, bf16[16,4,8,128]{3,2,1,0:T(8,128)(2,1)}, f32[3,3,16,64]{3,2,1,0:T(8,128)}, f32[3,3,3,16,64]{4,3,2,1,0:T(8,128)}) custom-call(bf16[4,16,8,128]{3,2,1,0:T(8,128)(2,1)} %bitcast.10, bf16[4,16,8,128]{3,2,1,0:T(8,128)(2,1)} %bitcast.11, f32[3,3,16,64]{3,2,1,0:T(8,128)} %copy-done.4, ...), custom_call_target="tpu_custom_call" | custom-call | tf_op jit(solution)/shard_map/pallas_call | solution.py:519
Async XLA Ops:
  0.6 1.0 %copy-start = (bf16[64,4,8,128]{3,2,1,0:T(8,128)(2,1)S(1)}, bf16[64,4,8,128]{3,2,1,0:T(8,128)(2,1)}, u32[]{:S(2)}) copy-start(bf16[64,4,8,128]{3,2,1,0:T(8,128)(2,1)} %volume.1) | copy-start | bytes 1572868
  1.7 0.9 %copy-start.2 = (bf16[16,4,8,128]{3,2,1,0:T(8,128)(2,1)S(1)}, bf16[16,4,8,128]{3,2,1,0:T(8,128)(2,1)}, u32[]{:S(2)}) copy-start(bf16[16,4,8,128]{3,2,1,0:T(8,128)(2,1)} %cotangent.1) | copy-start | bytes 393220
  2.6 0.9 %copy-start.3 = (bf16[3,3,3,16,64]{4,3,2,1,0:T(8,128)(2,1)S(1)}, bf16[3,3,3,16,64]{4,3,2,1,0:T(8,128)(2,1)}, u32[]{:S(2)}) copy-start(bf16[3,3,3,16,64]{4,3,2,1,0:T(8,128)(2,1)} %w_second.1) | copy-start | bytes 165892
  3.5 0.8 %copy-start.5 = (bf16[3,3,16,64]{3,2,1,0:T(8,128)(2,1)S(1)}, bf16[3,3,16,64]{3,2,1,0:T(8,128)(2,1)}, u32[]{:S(2)}) copy-start(bf16[3,3,16,64]{3,2,1,0:T(8,128)(2,1)} %w_first.1) | copy-start | bytes 55300
  32.9 0.6 %copy-start.4 = (f32[3,3,16,64]{3,2,1,0:T(8,128)}, f32[3,3,16,64]{3,2,1,0:T(8,128)S(1)}, u32[]{:S(2)}) copy-start(f32[3,3,16,64]{3,2,1,0:T(8,128)S(1)} %get-tuple-element.10.first) | copy-start | bytes 110596
  33.5 1.4 %copy-start.1 = (f32[3,3,3,16,64]{4,3,2,1,0:T(8,128)}, f32[3,3,3,16,64]{4,3,2,1,0:T(8,128)S(1)}, u32[]{:S(2)}) copy-start(f32[3,3,3,16,64]{4,3,2,1,0:T(8,128)S(1)} %get-tuple-element.11.second) | copy-start | bytes 331780

commit v4 on v3

--- a/solution.py
+++ b/solution.py
@@ -448,18 +448,6 @@
             gather(k, role).wait_send()
     first_sum[3]()
     second_sum[3]()
-
-
-def hand_out(out, inp, first, second, out_to, inp_to, first_to, second_to, sem):
-    z_cells = out.shape[0]
-    pairs = [(out.at[z], out_to.at[:, z]) for z in range(z_cells)]
-    pairs += [(inp.at[z], inp_to.at[:, z]) for z in range(z_cells)]
-    pairs += [(first, first_to), (second, second_to)]
-    copies = [pltpu.make_async_copy(s, t, sem.at[k]) for k, (s, t) in enumerate(pairs)]
-    for copy in copies:
-        copy.start()
-    for copy in copies:
-        copy.wait()
 
 
 def per_device(nb, nf, volume, w_first, w_second, cotangent):
@@ -512,22 +500,11 @@
             dma((2 * nb,)), dma((2 * nb,)), dma((2 * nb,)), dma((2 * nb,)),
         ],
         compiler_params=pltpu.CompilerParams(
-            collective_id=0, has_side_effects=True, vmem_limit_bytes=40 * 1024 * 1024
+            collective_id=0, has_side_effects=True, vmem_limit_bytes=64 * 1024 * 1024 - 512 * 1024
         ),
     )(volume, w_first, w_second, cotangent)
-    planes = (z_cells, own, y_rows, width)
-    output, input_grad, first, second = pl.pallas_call(
-        hand_out,
-        out_shape=(
-            jax.ShapeDtypeStruct(cotangent.shape, bf16),
-            jax.ShapeDtypeStruct(cotangent.shape, bf16),
-            jax.ShapeDtypeStruct(first.shape, f32),
-            jax.ShapeDtypeStruct(second.shape, f32),
-        ),
-        in_specs=[pl.BlockSpec(memory_space=pltpu.VMEM)] * 4,
-        out_specs=(pl.BlockSpec(memory_space=pltpu.HBM),) * 4,
-        scratch_shapes=[dma((2 * z_cells + 2,))],
-    )(out.reshape(planes), inp.reshape(planes), first, second)
+    output = out.reshape(z_cells, own, y_rows, width).transpose(1, 0, 2, 3)
+    input_grad = inp.reshape(z_cells, own, y_rows, width).transpose(1, 0, 2, 3)
     return (output, input_grad, first, second)
 
 

time: 37.2 us -> 33.5 us (0.901)
  local copies, waits for them, and re-layouts: 5.64 us -> 3.17 us
  Pallas kernels: 30.6 us -> 29.5 us
    unnamed x14 -> x10, local copies, waits for them, and re-layouts: 5.64 us -> 2.43 us
    pallas_call x1 -> x0, Pallas kernels: 1.98 us -> none  [per_device(): pl.pallas_call(hand_out, out_shape=(jax.ShapeDtypeStruct(cotangent.shape,...]
    pallas_call x1, Pallas kernels: 28.6 us -> 29.5 us  [per_device(): pl.pallas_call(functools.partial(kernel, (nb, nf, y_rows, width)), out_sh...]
    transpose x0 -> x1, local copies, waits for them, and re-layouts: none -> 0.75 us  [per_device(): input_grad = inp.reshape(z_cells, own, y_rows, width).transpose(1, 0, 2, 3)]
where the time goes in v4:
time: 33.5 us; the launch traced here: 33.4 us
  Pallas kernels  29.5 us (88%)
  local copies, waits for them, and re-layouts  3.17 us (9%)
  between operations  0.68 us (2%)
    pallas_call x1, Pallas kernels, per_device(): pl.pallas_call(functools.partial(kernel, (nb, nf, y_rows, width)), out_sh...  29.5 us
    unnamed x10, local copies, waits for them, and re-layouts  2.43 us
    transpose x1, local copies, waits for them, and re-layouts, per_device(): input_grad = inp.reshape(z_cells, own, y_rows, width).transpose(1, 0, 2, 3)  0.75 us

profile of v4, /device:TPU:0, one launch (start us, length us, event | category | flops | bytes accessed | tf_op | source)
XLA Modules:
  0.0 33.4 jit_solution(13213592890627628200)
XLA Ops:
  0.6 29.5 %shard_map.75 = (bf16[4,16,1024]{2,1,0:T(8,128)(2,1)}, bf16[4,16,1024]{2,1,0:T(8,128)(2,1)}, f32[3,3,16,64]{3,2,1,0:T(8,128)}, f32[3,3,3,16,64]{4,3,2,1,0:T(8,128)}) custom-call(bf16[64,4,8,128]{3,2,1,0:T(8,128)(2,1)} %volume.1, bf16[3,3,16,64]{3,2,1,0:T(8,128)(2,1)} %w_first.1, bf16[3,3,3,16,64]{4,3,2,1,0:T(8,128)(2,1)} %w_second.1, ...), custom_call_target="tpu_custom_call" | custom-call | tf_op jit(solution)/shard_map/pallas_call | solution.py:462
  30.1 0.0 copy-start.1
  30.1 1.0 %copy.10 = bf16[8,8,8,128]{3,2,1,0:T(8,128)(2,1)S(1)} copy(bf16[8,8,8,128]{3,1,2,0:T(8,128)(2,1)} %bitcast.23) | data formatting | bytes 262144
  31.1 0.0 copy-done.1
  31.2 0.0 copy-start.2
  31.2 0.0 copy-start
  31.2 0.7 %copy_bitcast_fusion = (bf16[16,4,8,128]{3,2,1,0:T(8,128)(2,1)}, bf16[16,4,8,128]{3,2,1,0:T(8,128)(2,1)}) fusion(bf16[4,16,8,128]{3,2,1,0:T(8,128)(2,1)S(1)} %bitcast.20, bf16[4,16,8,128]{3,2,1,0:T(8,128)(2,1)S(1)} %bitcast.21), kind=kLoop, calls=%fused_computation | loop fusion | bytes 524288 | tf_op jit(solution)/shard_map/transpose | solution.py:507
  31.9 0.1 copy-done.2
  32.0 0.6 %copy.16 = f32[3,3,16,64]{3,2,1,0:T(8,128)} copy(f32[3,3,16,64]{3,2,1,0:T(8,128)S(1)} %copy-done.2) | data formatting | bytes 73728
  32.7 0.0 copy-done
  32.7 0.7 %copy.17 = f32[3,3,3,16,64]{4,3,2,1,0:T(8,128)} copy(f32[3,3,3,16,64]{4,3,2,1,0:T(8,128)S(1)} %copy-done) | data formatting | bytes 221184
  (1 shorter events, 0.0 us)
Async XLA Ops:
  30.1 1.0 %copy-start.1 = (bf16[4,16,1024]{2,1,0:T(8,128)(2,1)S(1)}, bf16[4,16,1024]{2,1,0:T(8,128)(2,1)}, u32[]{:S(2)}) copy-start(bf16[4,16,1024]{2,1,0:T(8,128)(2,1)} %get-tuple-element.9) | copy-start | bytes 393220
  31.2 0.9 %copy-start.2 = (f32[3,3,16,64]{3,2,1,0:T(8,128)S(1)}, f32[3,3,16,64]{3,2,1,0:T(8,128)}, u32[]{:S(2)}) copy-start(f32[3,3,16,64]{3,2,1,0:T(8,128)} %get-tuple-element.20) | copy-start | bytes 110596
  31.2 1.5 %copy-start = (f32[3,3,3,16,64]{4,3,2,1,0:T(8,128)S(1)}, f32[3,3,3,16,64]{4,3,2,1,0:T(8,128)}, u32[]{:S(2)}) copy-start(f32[3,3,3,16,64]{4,3,2,1,0:T(8,128)} %get-tuple-element.21) | copy-start | bytes 331780
